TPU v7x, 32 devices: a whole 2x2x4 slice. The times are simulated.
32 devices in a mesh: row: 8 (over y, x, core), col: 4 (over z).
Axes of the slice: x: 2, y: 2, z: 4, core: 2. Of those that a mesh axis runs over, the one named last changes fastest.
Arguments:
- subgrid_pixels: float32 [4096, 2, 2, 1024], P(('row', 'col')), may hold values from -6 to 6
- tile_offsets: int32 [4096, 2], P(('row', 'col')), may hold values from 0 to 255, as said below
- station_pairs: int32 [4096, 2], P(('row', 'col')), may hold values from 0 to 511
- time_blocks: int32 [4096], P(('row', 'col')), may hold values from 0 to 1
- channel_blocks: int32 [4096], P(('row', 'col')), may hold values from 0 to 7
- valid_counts: int32 [32], P(('row', 'col')), may hold values from 64 to 128, as said below
- aterms: bfloat16 [512, 2, 2, 2, 1024], replicated, may hold values from -4 to 4
- channel_weights: float32 [8], replicated, may hold values from 0.5 to 2
Outputs:
- image: float32 [2, 8192, 8192], P(None, ('row', 'col'))
Inputs may be any that keep to these rules, and one draw needn't show every extreme that they name: `tile_offsets`: within the valid entries of one device's list, at most 8 subgrids lie in the grid block of any one device (rows 1024 r to 1024 (r + 1) - 1, columns 2048 c to 2048 (c + 1) - 1 of device index r * 4 + c), and some device's block receives exactly 8 valid subgrids from every device. `valid_counts`: entry d counts the valid subgrids of device d, which are the first slots of its list; some device's list is full.
All inputs are finite; a program needn't handle non-finite values.
Results may differ from a plain program's by a relative error of at most 0.0003.
Values sent between devices are 32-bit elements; how exact they have to be, the bound alone decides.
No kernel may reach another device: no remote copies, remote signals or barrier semaphores. Data moves between devices by JAX's collectives and lax.ppermute only.
A program may use at most 320 MiB of HBM per device.

v0:
```python
import math

import jax
import jax.numpy as jnp
from jax import lax
from jax.sharding import PartitionSpec as P

G = 8192
SUB = 32


EXACT = lax.Precision.HIGHEST


def phase_table(row_size, column_size, modulus):
    row_index = jnp.arange(row_size, dtype=jnp.int32)[:, None]
    column_index = jnp.arange(column_size, dtype=jnp.int32)[None, :]
    phase_angle = (
        -2.0 * math.pi / modulus * (row_index * column_index % modulus).astype(jnp.float32)
    )
    return (jnp.cos(phase_angle), jnp.sin(phase_angle))


def kron_table(subgrid_side):
    pixel_index = jnp.arange(subgrid_side * subgrid_side, dtype=jnp.int32)
    coarse_index = pixel_index // subgrid_side
    fine_index = pixel_index % subgrid_side
    turn_count = (
        coarse_index[:, None] * coarse_index[None, :] + fine_index[:, None] * fine_index[None, :]
    ) % subgrid_side
    phase_angle = -2.0 * math.pi / subgrid_side * turn_count.astype(jnp.float32)
    return (jnp.cos(phase_angle) / subgrid_side, jnp.sin(phase_angle) / subgrid_side)


def complex_einsum(formula, left_real, left_imag, right_real, right_imag):
    real_real = jnp.einsum(formula, left_real, right_real, precision=EXACT)
    imag_imag = jnp.einsum(formula, left_imag, right_imag, precision=EXACT)
    real_imag = jnp.einsum(formula, left_real, right_imag, precision=EXACT)
    imag_real = jnp.einsum(formula, left_imag, right_real, precision=EXACT)
    return (real_real - imag_imag, real_imag + imag_real)


def correct_subgrids(
    pixels, station_pair, time_index, channel_index, aterms, channel_weights, dft_real, dft_imag
):
    beam_first = aterms[station_pair[:, 0], time_index].astype(jnp.float32)
    beam_second = aterms[station_pair[:, 1], time_index].astype(jnp.float32)
    gain_real = beam_first[:, 0] * beam_second[:, 0] + beam_first[:, 1] * beam_second[:, 1]
    gain_imag = beam_first[:, 1] * beam_second[:, 0] - beam_first[:, 0] * beam_second[:, 1]
    matches = (
        channel_index[:, None] == jnp.arange(channel_weights.shape[0], dtype=jnp.int32)[None, :]
    )
    weight = jnp.sum(jnp.where(matches, channel_weights[None, :], 0.0), axis=1)[:, None, None]
    pixel_real = pixels[:, 0]
    pixel_imag = pixels[:, 1]
    fixed_real = (pixel_real * gain_real - pixel_imag * gain_imag) * weight
    fixed_imag = (pixel_real * gain_imag + pixel_imag * gain_real) * weight
    item_count = pixels.shape[0]
    feed_count = pixels.shape[2]
    pixel_count = pixels.shape[3]
    flat_real = fixed_real.reshape(item_count * feed_count, pixel_count)
    flat_imag = fixed_imag.reshape(item_count * feed_count, pixel_count)
    out_real = jnp.dot(flat_real, dft_real, precision=EXACT) - jnp.dot(
        flat_imag, dft_imag, precision=EXACT
    )
    out_imag = jnp.dot(flat_real, dft_imag, precision=EXACT) + jnp.dot(
        flat_imag, dft_real, precision=EXACT
    )
    return jnp.stack(
        [
            out_real.reshape(item_count, feed_count, pixel_count),
            out_imag.reshape(item_count, feed_count, pixel_count),
        ],
        axis=1,
    )


def local(
    subgrid_pixels,
    tile_offsets,
    station_pairs,
    time_blocks,
    channel_blocks,
    valid_counts,
    aterms,
    channel_weights,
):
    row_count = lax.axis_size("row")
    column_count = lax.axis_size("col")
    devices = row_count * column_count
    slot_count = subgrid_pixels.shape[0]
    capacity = 2 * slot_count // devices
    rows_dev = G // row_count
    cols_dev = G // column_count
    tile_rows = rows_dev // SUB
    tile_cols = cols_dev // SUB
    tiles_dev = tile_rows * tile_cols
    buffer_rows = devices * capacity
    dft_real, dft_imag = kron_table(SUB)
    slot_index = jnp.arange(slot_count, dtype=jnp.int32)
    is_valid = slot_index < valid_counts[0]
    tile_row = tile_offsets[:, 0]
    tile_column = tile_offsets[:, 1]
    owner_index = tile_row // tile_rows * column_count + tile_column // tile_cols
    local_tile = tile_row % tile_rows * tile_cols + tile_column % tile_cols
    earlier = (
        (owner_index[:, None] == owner_index[None, :])
        & (slot_index[None, :] < slot_index[:, None])
        & is_valid[None, :]
    )
    owner_rank = jnp.sum(earlier.astype(jnp.int32), axis=1)
    target = jnp.where(is_valid, owner_index * capacity + owner_rank, buffer_rows)
    details = jnp.stack(
        [local_tile, station_pairs[:, 0], station_pairs[:, 1], time_blocks, channel_blocks], axis=1
    ).astype(jnp.float32)
    blank_rows = jnp.zeros((buffer_rows, 5), jnp.float32).at[:, 0].set(float(tiles_dev))
    send_details = blank_rows.at[target].set(details, mode="drop")
    send_pixels = (
        jnp.zeros((buffer_rows,) + subgrid_pixels.shape[1:], jnp.float32)
        .at[target]
        .set(subgrid_pixels, mode="drop")
    )
    got_pixels, got_details = (
        lax.all_to_all(send_pixels, ("row", "col"), split_axis=0, concat_axis=0, tiled=True),
        lax.all_to_all(send_details, ("row", "col"), split_axis=0, concat_axis=0, tiled=True),
    )
    decoded = got_details.astype(jnp.int32)
    spectra = correct_subgrids(
        got_pixels,
        decoded[:, 1:3],
        decoded[:, 3],
        decoded[:, 4],
        aterms,
        channel_weights,
        dft_real,
        dft_imag,
    )
    tile_index = decoded[:, 0]
    summed = jax.ops.segment_sum(spectra, tile_index, num_segments=tiles_dev + 1)[:tiles_dev]
    uv_grid = (
        summed.reshape(tile_rows, tile_cols, 2, 2, SUB, SUB)
        .transpose(2, 3, 0, 4, 1, 5)
        .reshape(4, rows_dev, cols_dev)
    )
    stripe = rows_dev // column_count
    rows_block = lax.all_to_all(uv_grid, "col", split_axis=1, concat_axis=2, tiled=True)
    factor = G // 128
    shaped = rows_block.reshape(4, stripe, factor, 128)
    first_real, first_imag = phase_table(factor, factor, factor)
    mid_real, mid_imag = complex_einsum(
        "prba,kb->prka", shaped[:2], shaped[2:], first_real, first_imag
    )
    twist_real, twist_imag = phase_table(factor, 128, G)
    mid_real, mid_imag = (
        mid_real * twist_real - mid_imag * twist_imag,
        mid_real * twist_imag + mid_imag * twist_real,
    )
    second_real, second_imag = phase_table(128, 128, 128)
    out_real, out_imag = complex_einsum(
        "prka,wa->pwrk", mid_real, mid_imag, second_real, second_imag
    )
    spectrum = jnp.concatenate([out_real, out_imag], axis=0).reshape(4, devices, -1)
    spectrum = lax.all_to_all(spectrum, ("row", "col"), split_axis=1, concat_axis=1, tiled=True)
    spectrum_block = spectrum.reshape(4, devices, 128 // devices, stripe, factor)
    third_real, third_imag = phase_table(devices, devices, devices)
    high_real, high_imag = complex_einsum(
        "pjkuq,cj->pckuq", spectrum_block[:2], spectrum_block[2:], third_real, third_imag
    )
    turn_real, turn_imag = phase_table(devices, stripe, G)
    turn_real = turn_real[None, :, None, :, None]
    turn_imag = turn_imag[None, :, None, :, None]
    high_real, high_imag = (
        high_real * turn_real - high_imag * turn_imag,
        high_real * turn_imag + high_imag * turn_real,
    )
    last_real, last_imag = phase_table(stripe, stripe, stripe)
    image_scale = 1.0 / (SUB * math.sqrt(slot_count * devices))
    image = jnp.einsum("pckuq,wu->pkqwc", high_real, last_real, precision=EXACT) - jnp.einsum(
        "pckuq,wu->pkqwc", high_imag, last_imag, precision=EXACT
    )
    return image.reshape(2, 128 // devices * factor, G) * image_scale


def solution(mesh):
    in_specs = (
        P(("row", "col"), None, None, None),
        P(("row", "col"), None),
        P(("row", "col"), None),
        P(("row", "col")),
        P(("row", "col")),
        P(("row", "col")),
        P(),
        P(),
    )
    out_specs = P(None, ("row", "col"), None)
    return jax.shard_map(local, mesh=mesh, in_specs=in_specs, out_specs=out_specs, check_vma=False)
```

profile of v0, /device:TPU:0, one launch (start us, length us, event | category | flops | bytes accessed | tf_op | source)
XLA Modules:
  0.0 3007.6 jit_solution(15305691386749426677)
XLA Ops:
  79.8 52.3 %all-to-all-done.1 = f32[256,2,2,1024]{3,2,1,0:T(2,128)} async-done(((f32[256,2,2,1024]{3,2,1,0:T(2,128)}), f32[256,2,2,1024]{3,2,1,0:T(2,128)}, u32[]{:S(2)}, u32[]{:S(2)}) %all-to-all-start.1) | async-done | bytes 4194336 | tf_op jit(solution)/shard_map/all_to_all | solution.py:124
  149.4 25.0 fusion.22
  174.5 25.3 fusion.21
  199.8 25.5 fusion.37
  227.7 27.4 fusion.40
  275.5 43.7 %scatter_fusion.2 = f32[2049,2,2,1024]{3,2,1,0:T(2,128)} fusion(f32[2049,2,2,1024]{3,2,1,0:T(2,128)} %broadcast_in_dim.16, s32[256]{0:T(256)S(1)} %bitcast.149, f32[256,2,2,1024]{3,2,1,0:T(2,128)} %pad_maximum_fusion.1), kind=kCustom, calls=%fused_computation.4 | custom fusion | flops 1048576 | bytes 12583936 | tf_op jit(solution)/shard_map/scatter-add | solution.py:139
  342.0 48.7 %copy.117 = f32[2048,2,2,1024]{0,3,2,1:T(8,128)} copy(f32[2048,2,2,1024]{3,2,1,0:T(2,128)} %slice.127) | data formatting | bytes 67108864 | tf_op jit(solution)/shard_map/slice | solution.py:139
  390.7 54.2 %reshape.266 = f32[32,64,2,2,32,32]{1,0,5,4,3,2:T(8,128)} reshape(f32[2048,2,2,1024]{0,3,2,1:T(8,128)} %copy.117) | data formatting | bytes 67108864 | tf_op jit(solution)/shard_map/reshape | solution.py:141
  444.9 91.1 %copy.147 = f32[2,2,32,32,64,32]{5,4,1,0,3,2:T(8,128)} copy(f32[2,2,32,32,64,32]{4,2,5,3,1,0:T(8,128)} %bitcast.24) | data formatting | bytes 67108864 | tf_op jit(solution)/shard_map/reshape | solution.py:143
  536.0 101.1 %reshape.313 = f32[4,1024,2048]{2,0,1:T(4,128)} reshape(f32[2,2,32,32,64,32]{5,4,1,0,3,2:T(8,128)} %copy.147) | data formatting | bytes 67108864 | tf_op jit(solution)/shard_map/reshape | solution.py:143
  647.0 721.1 %all-to-all-done.2 = f32[4,1024,2048]{2,0,1:T(4,128)} async-done(((f32[4,1024,2048]{2,0,1:T(4,128)}), f32[4,1024,2048]{2,0,1:T(4,128)}, u32[]{:S(2)}, u32[]{:S(2)}) %all-to-all-start.2) | async-done | bytes 33554464 | tf_op jit(solution)/shard_map/all_to_all | solution.py:146
  1368.2 31.8 %copy.120 = f32[4,1024,2048]{2,1,0:T(8,128)} copy(f32[4,1024,2048]{2,0,1:T(4,128)} %all-to-all-done.2) | data formatting | bytes 67108864 | tf_op jit(solution)/shard_map/all_to_all | solution.py:146
  1566.0 36.2 %subtract_bitcast_fusion.2 = (f32[2,256,64,128]{3,2,1,0:T(8,128)}, f32[2,256,64,128]{3,2,1,0:T(8,128)}) fusion(f32[64,128]{1,0:T(8,128)S(1)} %get-tuple-element.36, f32[64,128]{1,0:T(8,128)S(1)} %get-tuple-element.37, f32[64,2,256,128]{3,0,2,1:T(8,128)} %fusion.84, f32[64,2,256,128]{3,0,2,1:T(8,128)} %fusion.80, f32[64,2,256,128]{3,0,2,1:T(8,128)} %fusion.82, ...), kind=kOutput, calls=%fused_computation.16 | convolution fusion | flops 3254837248 | bytes 100728832 | tf_op jit(solution)/shard_map/prba,kb->prka/dot_general | solution.py:37
  1602.2 33.0 %fusion.6 = f32[128,2,256,64]{2,0,3,1:T(8,128)} fusion(f32[2,256,64,128]{3,2,1,0:T(8,128)} %get-tuple-element.23), kind=kOutput, calls=%fused_computation.19 | convolution fusion | flops 6442680320 | bytes 33554432 | tf_op jit(solution)/shard_map/prka,wa->pwrk/dot_general | solution.py:37
  1635.3 32.4 %fusion.4 = f32[128,2,256,64]{2,0,3,1:T(8,128)} fusion(f32[2,256,64,128]{3,2,1,0:T(8,128)} %get-tuple-element.23), kind=kOutput, calls=%fused_computation.17 | convolution fusion | flops 6442680320 | bytes 33554432 | tf_op jit(solution)/shard_map/prka,wa->pwrk/dot_general | solution.py:39
  1667.6 34.8 %subtract_bitcast_fusion.1 = f32[2,128,256,64]{2,1,3,0:T(8,128)} fusion(f32[128,2,256,64]{2,0,3,1:T(8,128)} %fusion.6, f32[2,256,64,128]{3,2,1,0:T(8,128)} %get-tuple-element.22), kind=kOutput, calls=%fused_computation.14 | convolution fusion | flops 6446874624 | bytes 50331648 | tf_op jit(solution)/shard_map/prka,wa->pwrk/dot_general | solution.py:36
  1702.5 35.5 %add_bitcast_fusion.1 = f32[2,128,256,64]{2,1,3,0:T(8,128)} fusion(f32[128,2,256,64]{2,0,3,1:T(8,128)} %fusion.4, f32[2,256,64,128]{3,2,1,0:T(8,128)} %get-tuple-element.22), kind=kOutput, calls=%fused_computation.13 | convolution fusion | flops 6446874624 | bytes 50331648 | tf_op jit(solution)/shard_map/prka,wa->pwrk/dot_general | solution.py:38
  1738.0 23.1 pad_maximum_fusion
  1761.1 45.0 %copy.127 = f32[4,128,256,64]{3,2,1,0:T(8,128)} copy(f32[4,128,256,64]{2,1,3,0:T(8,128)} %pad_maximum_fusion) | data formatting | bytes 67108864 | tf_op jit(solution)/shard_map/concatenate | solution.py:162
  1806.2 40.4 %reshape.268 = f32[4,32,65536]{2,1,0:T(8,128)} reshape(f32[4,128,256,64]{3,2,1,0:T(8,128)} %copy.127) | data formatting | bytes 67108864 | tf_op jit(solution)/shard_map/reshape | solution.py:162
  1846.6 37.9 %copy.128 = f32[4,32,65536]{2,0,1:T(4,128)} copy(f32[4,32,65536]{2,1,0:T(8,128)} %reshape.268) | data formatting | bytes 67108864 | tf_op jit(solution)/shard_map/reshape | solution.py:162
  1889.3 720.5 %all-to-all-done.3 = f32[4,32,65536]{2,0,1:T(4,128)} async-done(((f32[4,32,65536]{2,0,1:T(4,128)}), f32[4,32,65536]{2,0,1:T(4,128)}, u32[]{:S(2)}, u32[]{:S(2)}) %all-to-all-start.3) | async-done | bytes 33554464 | tf_op jit(solution)/shard_map/all_to_all | solution.py:163
  2609.9 33.0 %fusion.228 = (f32[2,32,65536]{2,0,1:T(2,128)}, f32[2,32,65536]{2,0,1:T(2,128)}) fusion(f32[4,32,65536]{2,0,1:T(4,128)} %all-to-all-done.3), kind=kLoop, calls=%fused_computation.279 | loop fusion | bytes 67108864 | tf_op jit(solution)/shard_map/slice | solution.py:167
  2642.8 34.5 %reshape.314 = f32[2,32,4,256,64]{4,3,2,0,1:T(8,128)} reshape(f32[2,32,65536]{2,0,1:T(2,128)} %get-tuple-element.25) | data formatting | bytes 33554432 | tf_op jit(solution)/shard_map/slice | solution.py:167
  2677.3 26.3 copy.130
  2747.0 34.5 %reshape.315 = f32[2,32,4,256,64]{4,3,2,0,1:T(8,128)} reshape(f32[2,32,65536]{2,0,1:T(2,128)} %get-tuple-element.24) | data formatting | bytes 33554432 | tf_op jit(solution)/shard_map/slice | solution.py:167
  2781.5 26.3 copy.132
  2829.8 35.4 %subtract_bitcast_fusion = (f32[2,32,4,256,64]{3,1,4,2,0:T(8,128)}, f32[2,32,4,256,64]{3,1,4,2,0:T(8,128)}) fusion(f32[32,256]{1,0:T(8,128)S(1)} %get-tuple-element.38, f32[32,256]{1,0:T(8,128)S(1)} %get-tuple-element.39, f32[32,2,4,256,64]{3,0,4,2,1:T(8,128)} %fusion.110, f32[32,2,4,256,64]{3,0,4,2,1:T(8,128)} %fusion.106, ...), kind=kOutput, calls=%fused_computation.12 | convolution fusion | flops 1644181504 | bytes 100728832 | tf_op jit(solution)/shard_map/pjkuq,cj->pckuq/dot_general | solution.py:37
  2865.2 30.8 %fusion = f32[256,2,32,4,64]{0,4,3,2,1:T(8,128)} fusion(f32[2,32,4,256,64]{3,1,4,2,0:T(8,128)} %get-tuple-element.21), kind=kOutput, calls=%fused_computation.6 | convolution fusion | flops 12885819392 | bytes 33554432 | tf_op jit(solution)/shard_map/pckuq,wu->pkqwc/dot_general | solution.py:178
  2896.0 32.3 %multiply_bitcast_fusion = f32[2,4,64,256,32]{3,2,1,4,0:T(8,128)} fusion(f32[256,2,32,4,64]{0,4,3,2,1:T(8,128)} %fusion, f32[2,32,4,256,64]{3,1,4,2,0:T(8,128)} %get-tuple-element.20), kind=kOutput, calls=%fused_computation.10 | convolution fusion | flops 12894208000 | bytes 50331648 | tf_op jit(solution)/shard_map/pckuq,wu->pkqwc/dot_general | solution.py:178
  2928.3 31.1 %copy.137 = f32[2,4,64,256,32]{2,1,4,3,0:T(4,128)} copy(f32[2,4,64,256,32]{3,2,1,4,0:T(8,128)} %multiply_bitcast_fusion) | data formatting | bytes 33554432 | tf_op jit(solution)/shard_map/mul | solution.py:181
  2959.4 30.5 %mul.599 = f32[2,256,8192]{1,2,0:T(8,128)} reshape(f32[2,4,64,256,32]{2,1,4,3,0:T(4,128)} %copy.137) | data formatting | bytes 33554432 | tf_op jit(solution)/shard_map/mul | solution.py:181
  (61 shorter events, 405.0 us)
Async XLA Ops:
  0.0 18.0 copy-start
  6.5 27.0 all-to-all-start
  33.5 98.5 %all-to-all-start.1 = ((f32[256,2,2,1024]{3,2,1,0:T(2,128)}), f32[256,2,2,1024]{3,2,1,0:T(2,128)}, u32[]{:S(2)}, u32[]{:S(2)}) async-start(f32[256,2,2,1024]{3,2,1,0:T(2,128)} %scatter_fusion.1), calls=%async_computation.1 | async-start | bytes 8388608 | tf_op jit(solution)/shard_map/all_to_all | solution.py:124
  75.0 4.4 copy-start.2
  149.4 25.1 copy-start.1
  637.1 731.0 %all-to-all-start.2 = ((f32[4,1024,2048]{2,0,1:T(4,128)}), f32[4,1024,2048]{2,0,1:T(4,128)}, u32[]{:S(2)}, u32[]{:S(2)}) async-start(f32[4,1024,2048]{2,0,1:T(4,128)} %reshape.313), calls=%async_computation.2 | async-start | bytes 67108864 | tf_op jit(solution)/shard_map/all_to_all | solution.py:146
  1884.4 725.4 %all-to-all-start.3 = ((f32[4,32,65536]{2,0,1:T(4,128)}), f32[4,32,65536]{2,0,1:T(4,128)}, u32[]{:S(2)}, u32[]{:S(2)}) async-start(f32[4,32,65536]{2,0,1:T(4,128)} %copy.128), calls=%async_computation.3 | async-start | bytes 67108864 | tf_op jit(solution)/shard_map/all_to_all | solution.py:163
where the time goes:
time: 3050 us; the launch traced here: 3010 us
  waiting for transfers between devices  1490 us (49%)
  local copies, waits for them, and re-layouts  882 us (29%)
  matrix products  505 us (17%)
  other arithmetic  96.3 us (3%)
    all_to_all x1, waiting for transfers between devices, local(): lax.all_to_all(uv_grid, 'col', split_axis=1, concat_axis=2, tiled=True)  721 us
    all_to_all x1, waiting for transfers between devices, local(): lax.all_to_all(spectrum, ('row', 'col'), split_axis=1, concat_axis=1, til...  721 us
    reshape x2, local copies, waits for them, and re-layouts, local(): uv_grid = summed.reshape(tile_rows, tile_cols, 2, 2, SUB, SUB).transpose(...  192 us
    dot_general x3, matrix products, complex_einsum(): imag_imag = jnp.einsum(formula, left_imag, right_imag, precision=EXACT)  105 us
    slice x3, local copies, waits for them, and re-layouts, local(): spectrum_block[2:]  93.7 us
    dot_general x3, matrix products, complex_einsum(): real_imag = jnp.einsum(formula, left_real, right_imag, precision=EXACT)  79.2 us
    mul x3, local copies, waits for them, and re-layouts, local(): return image.reshape(2, 128 // devices * factor, G) * image_scale  79 us
    dot_general x3, matrix products, complex_einsum(): real_real = jnp.einsum(formula, left_real, right_real, precision=EXACT)  78.6 us
  transfers between devices with their start and end apart: 4, of which 3 were waited for; matrix products, arithmetic and copies ran while one was open for 2% of the time, Pallas kernels for 0%

commit v1 on v0

v1 whole, which is shorter than its diff:
```python
import math

import jax
import jax.numpy as jnp
import numpy as np
from jax import lax
from jax.experimental import pallas as pl
from jax.experimental.pallas import tpu as pltpu
from jax.sharding import PartitionSpec as P

G = 8192
SUB = 32
TILES = G // SUB
HALF = 2 * SUB
AXES = ("row", "col")
GROUP = 8
IN_FLIGHT = 4
VMEM_LIMIT = 60 * 1024 * 1024


def split(value):
    high = lax.reduce_precision(value, 8, 7)
    return high.astype(jnp.bfloat16), (value - high).astype(jnp.bfloat16)


def subgrid_table():
    index = np.arange(SUB)
    turns = (
        index[:, None, None, None] * index[None, None, :, None]
        + index[None, :, None, None] * index[None, None, None, :]
    ) % SUB
    wave = np.exp(-2j * np.pi / SUB * turns) / SUB
    table = np.zeros((2, SUB, SUB, SUB, 2, SUB))
    table[0, :, :, :, 0, :] = wave.real
    table[0, :, :, :, 1, :] = wave.imag
    table[1, :, :, :, 0, :] = -wave.imag
    table[1, :, :, :, 1, :] = wave.real
    table = table.reshape(2 * SUB * SUB, 2 * SUB * SUB).astype(np.float32)
    high = table.astype(jnp.bfloat16)
    low = (table - high.astype(np.float32)).astype(jnp.bfloat16)
    return high, low


def spectra_of(pixels, pairs, times, channels, valid, aterms, weights):
    slots = pixels.shape[0]
    first = aterms[pairs[:, 0], times].astype(jnp.float32)
    second = aterms[pairs[:, 1], times].astype(jnp.float32)
    gain_real = first[:, 0] * second[:, 0] + first[:, 1] * second[:, 1]
    gain_imag = first[:, 1] * second[:, 0] - first[:, 0] * second[:, 1]
    matches = channels[:, None] == jnp.arange(weights.shape[0], dtype=jnp.int32)[None, :]
    weight = jnp.sum(jnp.where(matches, weights[None, :], 0.0), axis=1)
    weight = jnp.where(valid, weight, 0.0)[:, None, None]
    real = (pixels[:, 0] * gain_real - pixels[:, 1] * gain_imag) * weight
    imag = (pixels[:, 0] * gain_imag + pixels[:, 1] * gain_real) * weight
    fixed = jnp.stack([real, imag], axis=2).reshape(slots * 2, 2 * SUB * SUB)
    table_high, table_low = subgrid_table()
    high, low = split(fixed)
    dot = lambda left, right: jnp.dot(left, right, preferred_element_type=jnp.float32)
    out = dot(high, table_high) + dot(low, table_high) + dot(high, table_low)
    return out.reshape(slots, 2 * SUB // 2, 128)


def phases(turns, modulus):
    angle = (2.0 * math.pi / modulus) * (turns % modulus).astype(jnp.float32)
    return jnp.cos(angle), jnp.sin(angle)


def column_tables(first_m, lanes):
    m = first_m + jnp.arange(lanes, dtype=jnp.int32)
    cos, sin = phases(jnp.arange(SUB, dtype=jnp.int32)[:, None] * m[None, :], G)
    table = jnp.concatenate(
        [jnp.concatenate([cos, -sin], axis=1), jnp.concatenate([sin, cos], axis=1)], axis=0
    )
    high, low = split(table)
    table = jnp.concatenate([high, high, low, jnp.zeros_like(high)], axis=0)
    cos, sin = phases(jnp.arange(TILES, dtype=jnp.int32)[:, None] * m[None, :], TILES)
    turn = jnp.concatenate([cos, -sin], axis=1)
    return table, jnp.broadcast_to(turn[:, None, :], (TILES, 8, 2 * lanes))


def row_table():
    b = jnp.arange(TILES, dtype=jnp.int32)
    u = jnp.arange(SUB, dtype=jnp.int32)
    cos_r, sin_r = phases(b[:, None] * b[None, :], TILES)
    u = u % (SUB // 2) * 2 + u // (SUB // 2)
    cos_u, sin_u = phases(u[:, None] * b[None, :], G)
    cos = cos_r[None] * cos_u[:, :, None] - sin_r[None] * sin_u[:, :, None]
    sin = sin_r[None] * cos_u[:, :, None] + cos_r[None] * sin_u[:, :, None]
    high, low = split(jnp.concatenate([-sin, cos, sin], axis=2))
    return jnp.stack([high, low], axis=1)


def gather_kernel(
    codes, counts, slot_start, x_ref, table_ref, turn_ref, held_ref, out_ref, total, mid, sem, *, first, lanes
):
    step = pl.program_id(0)

    @pl.when(step == 0)
    def _():
        if first:
            total[...] = jnp.zeros_like(total)
        else:
            copy = pltpu.make_async_copy(held_ref, total, sem)
            copy.start()
            copy.wait()

    per_step = x_ref.shape[0]
    is_low = lax.broadcasted_iota(jnp.int32, (GROUP * SUB, 128), 1) < HALF
    for group in range(per_step // GROUP):
        start = group * GROUP

        @pl.when(slot_start + start < counts[step])
        def _():
            x = x_ref[start : start + GROUP].reshape(GROUP * SUB, 128)
            high = x.astype(jnp.bfloat16).astype(jnp.float32)
            low = x - high
            high_turned = pltpu.roll(high, HALF, 1)
            low_turned = pltpu.roll(low, HALF, 1)
            sides = (
                (jnp.where(is_low, high, low_turned), high),
                (jnp.where(is_low, high_turned, low), high_turned),
            )
            for parity, (mixed, other) in enumerate(sides):
                left = jnp.concatenate(
                    [mixed.astype(jnp.bfloat16), other.astype(jnp.bfloat16)], axis=1
                )
                mid[parity] = jnp.dot(left, table_ref[...], preferred_element_type=jnp.float32)
            for item in range(GROUP):
                code = codes[step * per_step + start + item]
                row = code // TILES
                column = code % TILES
                for tile in range(lanes // 128):
                    here = slice(tile * 128, (tile + 1) * 128)
                    there = slice(lanes + tile * 128, lanes + (tile + 1) * 128)
                    turn_real = turn_ref[column, :, here][None]
                    turn_imag = turn_ref[column, :, there][None]
                    for parity in range(2):
                        piece = slice(item * SUB, (item + 1) * SUB)
                        real = mid[parity, piece, here].reshape(SUB // 8, 8, 128)
                        imag = mid[parity, piece, there].reshape(SUB // 8, 8, 128)
                        rows = slice(parity * SUB, (parity + 1) * SUB)
                        total[row, tile, rows] += (real * turn_real - imag * turn_imag).reshape(
                            SUB, 128
                        )
                        total[row, lanes // 128 + tile, rows] += (
                            real * turn_imag + imag * turn_real
                        ).reshape(SUB, 128)

    @pl.when(step == pl.num_programs(0) - 1)
    def _():
        copy = pltpu.make_async_copy(total, out_ref, sem)
        copy.start()
        copy.wait()


def add_columns(chunk, codes, counts, slot_start, table, turn, held, lanes):
    sources = counts.shape[0]
    per_source = chunk.shape[0] // sources
    shape = (TILES, 2 * lanes // 128, 2 * SUB, 128)
    first = held is None
    if first:
        held = jnp.zeros((8, 128), jnp.float32)

    def kernel(*refs):
        gather_kernel(refs[0], refs[1], slot_start, *refs[2:], first=first, lanes=lanes)

    return pl.pallas_call(
        kernel,
        out_shape=jax.ShapeDtypeStruct(shape, jnp.float32),
        grid_spec=pltpu.PrefetchScalarGridSpec(
            num_scalar_prefetch=2,
            grid=(sources,),
            in_specs=[
                pl.BlockSpec((per_source, SUB, 128), lambda i, *_: (i, 0, 0)),
                pl.BlockSpec(table.shape, lambda i, *_: (0, 0)),
                pl.BlockSpec(turn.shape, lambda i, *_: (0, 0, 0)),
                pl.BlockSpec(memory_space=pl.ANY),
            ],
            out_specs=pl.BlockSpec(memory_space=pl.ANY),
            scratch_shapes=[
                pltpu.VMEM(shape, jnp.float32),
                pltpu.VMEM((2, GROUP * SUB, 2 * lanes), jnp.float32),
                pltpu.SemaphoreType.DMA,
            ],
        ),
        input_output_aliases={} if first else {5: 0},
        compiler_params=pltpu.CompilerParams(
            vmem_limit_bytes=VMEM_LIMIT, dimension_semantics=("arbitrary",)
        ),
        cost_estimate=pl.CostEstimate(
            flops=chunk.shape[0] * HALF * 256 * 2 * lanes * 2 * 2,
            bytes_accessed=chunk.size * 4 + math.prod(shape) * 8,
            transcendentals=0,
        ),
    )(codes, counts, chunk, table, turn, held)


def real_transform(real, imag, size):
    if size == 2:
        return [real[0] + real[1], real[0] - real[1]]
    half = size // 2
    quarter = half // 2
    even = real_transform(real[::2], imag[::2], half)
    odd_indices = list(range(1, half, 2))

    def total(terms, a, wave):
        result = None
        for k in odd_indices:
            factor = wave(2.0 * math.pi * k * a / size)
            if abs(factor) < 1e-9:
                continue
            term = terms[k] * factor if abs(factor - 1.0) > 1e-9 else terms[k]
            result = term if result is None else result + term
        return result

    cosines = [total(real, a, math.cos) for a in range(quarter)] + [None]
    sines = [None] + [total(imag, a, math.sin) for a in range(1, quarter + 1)]
    odd = [None] * half
    for a in range(quarter + 1):
        if cosines[a] is None:
            odd[a] = sines[a]
        elif sines[a] is None:
            odd[a] = cosines[a]
        else:
            odd[a] = cosines[a] + sines[a]
            odd[half - a] = sines[a] - cosines[a]
    return [even[a] + odd[a] for a in range(half)] + [even[a] - odd[a] for a in range(half)]


def image_kernel(rows_ref, table_ref, out_ref, mid, *, lanes, scale):
    step = pl.program_id(1)
    tiles = 2 * lanes // 128
    rows = rows_ref.reshape(TILES * tiles * 8, 128)
    take = lambda tile: rows[pl.ds(tile * 8 + step % 8, TILES, tiles * 8), :]
    real = jnp.concatenate([take(tile) for tile in range(tiles // 2)], axis=1)
    imag = jnp.concatenate([take(tile) for tile in range(tiles // 2, tiles)], axis=1)
    data = jnp.concatenate([real, imag], axis=0)
    high = data.astype(jnp.bfloat16)
    low = (data - high.astype(jnp.float32)).astype(jnp.bfloat16)
    dot = lambda left, right: jnp.dot(left, right, preferred_element_type=jnp.float32)
    for part, columns in enumerate((slice(TILES, 3 * TILES), slice(0, 2 * TILES))):
        table_high = table_ref[0, 0, :, columns]
        table_low = table_ref[0, 1, :, columns]
        mid[step, part] = dot(table_high, high) + dot(table_low, high) + dot(table_high, low)

    @pl.when(step == SUB - 1)
    def _():
        place = lambda u: u % 2 * (SUB // 2) + u // 2

        def transform(b_tile, carry):
            where = pl.ds(pl.multiple_of(b_tile * 8, 8), 8)
            for lane in range(lanes // 128):
                at = slice(lane * 128, (lane + 1) * 128)
                take = lambda u, part: mid[place(u), part, where, at]
                real = [take(0, 0)]
                imag = [None]
                for u in range(1, SUB // 2):
                    real.append(take(u, 0) + take(SUB - u, 0))
                    imag.append(take(u, 1) - take(SUB - u, 1))
                real.append(take(SUB // 2, 0))
                imag.append(None)
                for a, value in enumerate(real_transform(real, imag, SUB)):
                    mid[a, 0, where, at] = value * scale
            return carry

        lax.fori_loop(0, TILES // 8, transform, 0)
        wanted = out_ref.shape[1]

        for a in range(SUB):
            out_ref[0, :, a * TILES : (a + 1) * TILES] = mid[a, 0].T[:wanted]


def make_image(rows, table, lanes, wanted, scale):
    def kernel(*refs):
        image_kernel(*refs, lanes=lanes, scale=scale)

    return pl.pallas_call(
        kernel,
        out_shape=jax.ShapeDtypeStruct((2, wanted, G), jnp.float32),
        grid=(2, SUB),
        in_specs=[
            pl.BlockSpec(
                (TILES, 2 * lanes // 128, 8, 128),
                lambda f, i: (0, 0, i // 16 * 4 + f * 2 + i % 16 // 8, 0),
            ),
            pl.BlockSpec((1,) + table.shape[1:], lambda f, i: (i, 0, 0, 0)),
        ],
        out_specs=pl.BlockSpec((1, wanted, G), lambda f, i: (f, 0, 0)),
        scratch_shapes=[pltpu.VMEM((SUB, 2, TILES, lanes), jnp.float32)],
        compiler_params=pltpu.CompilerParams(
            vmem_limit_bytes=VMEM_LIMIT, dimension_semantics=("arbitrary", "arbitrary")
        ),
        cost_estimate=pl.CostEstimate(
            flops=2 * SUB * 3 * 2 * 512 * 512 * lanes,
            bytes_accessed=rows.size * 4 + table.size * 4 + 2 * wanted * G * 4,
            transcendentals=0,
        ),
    )(rows, table)


def local(
    subgrid_pixels,
    tile_offsets,
    station_pairs,
    time_blocks,
    channel_blocks,
    valid_counts,
    aterms,
    channel_weights,
):
    devices = lax.axis_size("row") * lax.axis_size("col")
    slots = subgrid_pixels.shape[0]
    wanted = G // devices
    lanes = max(wanted, 128)
    first_m = (lax.axis_index("row") * lax.axis_size("col") + lax.axis_index("col")) * wanted
    chunks = max(4, slots * devices // 1024)
    per_chunk = slots // chunks

    valid = jnp.arange(slots, dtype=jnp.int32) < valid_counts[0]
    codes = jnp.where(valid, tile_offsets[:, 0] * TILES + tile_offsets[:, 1], 0)
    small = jnp.concatenate([codes, jnp.broadcast_to(valid_counts, (128,))])
    small = lax.all_gather(small, AXES, tiled=True).reshape(devices, slots + 128)
    codes = small[:, :slots].reshape(devices, chunks, per_chunk)
    counts = small[:, slots]

    spectra = spectra_of(
        subgrid_pixels, station_pairs, time_blocks, channel_blocks, valid, aterms, channel_weights
    )
    table, turn = column_tables(first_m, lanes)
    rows = None
    gather = lambda part: lax.all_gather(part, AXES, tiled=True)
    parts = [spectra[chunk * per_chunk : (chunk + 1) * per_chunk] for chunk in range(chunks)]
    got = [gather(part) for part in parts[:IN_FLIGHT]]
    for chunk in range(chunks):
        rows = add_columns(
            got[chunk],
            codes[:, chunk].reshape(-1),
            counts,
            chunk * per_chunk,
            table,
            turn,
            rows,
            lanes,
        )
        if chunk + IN_FLIGHT < chunks:
            part, rows = lax.optimization_barrier((parts[chunk + IN_FLIGHT], rows))
            got.append(gather(part))
    scale = 1.0 / (SUB * math.sqrt(slots * devices))
    return make_image(rows, row_table(), lanes, wanted, scale)


def solution(mesh):
    in_specs = (
        P(AXES, None, None, None),
        P(AXES, None),
        P(AXES, None),
        P(AXES),
        P(AXES),
        P(AXES),
        P(),
        P(),
    )
    out_specs = P(None, AXES, None)
    return jax.shard_map(local, mesh=mesh, in_specs=in_specs, out_specs=out_specs, check_vma=False)
```

time: 3050 us -> 658 us (0.22); the launches traced: 3010 us -> 656 us
  waiting for transfers between devices: 1490 us -> 127 us
  local copies, waits for them, and re-layouts: 882 us -> 27.7 us
  matrix products: 505 us -> 7.2 us
  Pallas kernels: 0 us -> 372 us
  blocking collectives: 0 us -> 70.7 us
  other arithmetic: 96.3 us -> 37.7 us
    all_to_all x4 -> x0, waiting for transfers between devices: 1490 us -> none  [the longest x1 721 us: local(): lax.all_to_all(uv_grid, 'col', split_axis=1, concat_axis=2, tiled=True)]
    dot_general x18 -> x3, matrix products: 505 us -> 7.2 us  [spectra_of(): jnp.dot(left, right, preferred_element_type=jnp.float32)]
    pallas_call x0 -> x5, Pallas kernels: none -> 372 us  [the longest x4 278 us: add_columns(): pl.pallas_call(kernel, out_shape=jax.ShapeDtypeStruct(shape, jnp.float32)...]
    reshape x5 -> x1, local copies, waits for them, and re-layouts: 325 us -> 0.09 us  [local(): codes = small[:, :slots].reshape(devices, chunks, per_chunk)]
    slice x12 -> x9, local copies, waits for them, and re-layouts: 326 us -> 6.63 us  [the longest x5 3.72 us: local(): spectra[chunk * per_chunk:(chunk + 1) * per_chunk]]
    all_gather x0 -> x4, waiting for transfers between devices: none -> 126 us  [local(): gather = lambda part: lax.all_gather(part, AXES, tiled=True)]
    mul x5 -> x0, local copies, waits for them, and re-layouts: 79.3 us -> none  [the longest x3 79 us: local(): return image.reshape(2, 128 // devices * factor, G) * image_scale]
    all_gather x0 -> x1, blocking collectives: none -> 70.7 us  [local(): lax.all_gather(small, AXES, tiled=True).reshape(devices, slots + 128)]
  transfers between devices with their start and end apart: 4 -> 4, of which waited for: 3 -> 4; matrix products, arithmetic and copies ran while one was open for 2% -> 7% of each run, Pallas kernels for 0% -> 34%
where the time goes in v1:
time: 658 us; the launch traced here: 656 us
  Pallas kernels  372 us (57%)
  waiting for transfers between devices  127 us (19%)
  blocking collectives  70.7 us (11%)
  other arithmetic  37.7 us (6%)
  local copies, waits for them, and re-layouts  27.7 us (4%)
  between operations  14.1 us (2%)
  matrix products  7.2 us (1%)
    pallas_call x4, Pallas kernels, add_columns(): pl.pallas_call(kernel, out_shape=jax.ShapeDtypeStruct(shape, jnp.float32)...  278 us
    all_gather x4, waiting for transfers between devices, local(): gather = lambda part: lax.all_gather(part, AXES, tiled=True)  126 us
    pallas_call x1, Pallas kernels, make_image(): pl.pallas_call(kernel, out_shape=jax.ShapeDtypeStruct((2, wanted, G), jnp...  94.1 us
    all_gather x1, blocking collectives, local(): lax.all_gather(small, AXES, tiled=True).reshape(devices, slots + 128)  70.7 us
  transfers between devices with their start and end apart: 4, of which 4 were waited for; matrix products, arithmetic and copies ran while one was open for 7% of the time, Pallas kernels for 34%

profile of v1, /device:TPU:0, one launch (start us, length us, event | category | flops | bytes accessed | tf_op | source)
XLA Modules:
  0.0 655.9 jit_solution(17330474784395912055)
XLA Ops:
  6.5 0.8 fusion.50
  7.3 6.2 gather_fusion
  13.5 6.2 gather_fusion.1
  20.4 2.3 fusion.52
  22.6 0.8 copy_convert_fusion
  23.5 1.1 bitcast_multiply_fusion.1
  25.5 1.6 copy.97
  27.1 0.9 copy.110
  28.3 2.5 fusion.4
  30.8 2.3 convolution_add_fusion.1
  33.2 2.3 convolution_add_fusion
  35.7 0.9 slice.101
  36.7 0.9 slice.98
  37.6 0.9 slice.95
  38.6 0.9 slice.92
  39.5 70.7 %all-gather = s32[32,1,256]{2,1,0:T(1,128)S(1)} all-gather(s32[1,1,256]{2,1,0:T(1,128)S(1)} %bitcast.62), channel_id=1, replica_groups=mesh['row'=8,'col'=4] {'row','col'}, dimensions={0}, use_global_device_ids=true | all-gather | bytes 33792 | tf_op jit(solution)/shard_map/all_gather | solution.py:322
  113.9 1.0 fusion.18
  114.9 1.0 fusion.20
  116.3 0.8 maximum_maximum_fusion.refs_3_
  117.1 9.0 %negate_bitcast_fusion = (f32[32,1,256,256]{3,2,1,0:T(8,128)}, f32[32,1,256,256]{3,2,1,0:T(8,128)}, f32[32,1,256,256]{3,2,1,0:T(8,128)}) fusion(f32[32,256]{1,0:T(8,128)S(1)} %get-tuple-element.33, f32[256,256]{1,0:T(8,128)S(1)} %get-tuple-element.36, f32[32,256]{1,0:T(8,128)S(1)} %get-tuple-element.32, f32[256,256]{1,0:T(8,128)S(1)} %get-tuple-element.37), kind=kLoop, calls=%fused_computation.8 | loop fusion | flops 14680064 | bytes 25755648 | tf_op jit(solution)/shard_map/concatenate | solution.py:89
  126.1 11.3 %reduce-precision_convert_fusion = (bf16[32,1,256,768]{3,2,1,0:T(8,128)(2,1)S(1)}, bf16[32,1,256,768]{3,2,1,0:T(8,128)(2,1)S(1)}) fusion(f32[32,1,256,256]{3,2,1,0:T(8,128)} %get-tuple-element.18, f32[32,1,256,256]{3,2,1,0:T(8,128)} %get-tuple-element.17, f32[32,1,256,256]{3,2,1,0:T(8,128)} %get-tuple-element.16), kind=kLoop, calls=%fused_computation.3 | loop fusion | flops 37748736 | bytes 50331648 | tf_op jit(solution)/shard_map/convert_element_type | solution.py:23
  137.4 10.5 %pad_maximum_fusion.1.refs_1_ = bf16[32,2,256,768]{3,2,1,0:T(8,128)(2,1)} fusion(bf16[32,1,256,768]{3,2,1,0:T(8,128)(2,1)S(1)} %get-tuple-element.9, bf16[32,1,256,768]{3,2,1,0:T(8,128)(2,1)S(1)} %get-tuple-element.8), kind=kLoop, calls=%fused_computation.6 | loop fusion | flops 12582912 | bytes 50331648 | tf_op jit(solution)/shard_map/stack | solution.py:90
  147.9 6.7 %all-gather.12.cloned.1.call-done.refs_2_ = f32[1024,32,128]{2,1,0:T(8,128)} async-done(((f32[32,32,128]{2,1,0:T(8,128)}), f32[1024,32,128]{2,1,0:T(8,128)}) %all-gather.12.cloned.1.call-update) | async-done | bytes 16777232 | tf_op jit(solution)/shard_map/all_gather | solution.py:331
  154.6 2.6 broadcast_in_dim.37.refs_4_
  157.8 72.1 %shard_map.100.refs_5_ = f32[256,4,64,128]{3,2,1,0:T(8,128)} custom-call(s32[1024]{0:T(1024)} %reshape_squeeze.15.refs_0_, s32[32]{0:T(128)} %slice_reduce_fusion.refs_1_, f32[1024,32,128]{2,1,0:T(8,128)} %all-gather.12.cloned.1.call-done.refs_2_, bf16[256,512]{1,0:T(8,128)(2,1)} %maximum_maximum_fusion.refs_3_, f32[256,8,512]{2,1,0:T(8,128)} %broadcast_in_dim.37.refs_4_, ...), custom_call_target="tpu_custom_call" | custom-call | flops 34359738368 | bytes 83886080 | tf_op jit(solution)/shard_map/pallas_call | solution.py:167
  229.9 40.8 %all-gather.10.cloned.1.call-done.refs_2_ = f32[1024,32,128]{2,1,0:T(8,128)} async-done(((f32[32,32,128]{2,1,0:T(8,128)}), f32[1024,32,128]{2,1,0:T(8,128)}) %all-gather.10.cloned.1.call-update) | async-done | bytes 16777232 | tf_op jit(solution)/shard_map/all_gather | solution.py:331
  270.7 78.7 %shard_map.101.refs_5_ = f32[256,4,64,128]{3,2,1,0:T(8,128)} custom-call(s32[1024]{0:T(1024)} %reshape_squeeze.14.refs_0_, s32[32]{0:T(128)} %slice_reduce_fusion.refs_1_, f32[1024,32,128]{2,1,0:T(8,128)} %all-gather.10.cloned.1.call-done.refs_2_, bf16[256,512]{1,0:T(8,128)(2,1)} %maximum_maximum_fusion.refs_3_, ...), custom_call_target="tpu_custom_call", output_to_operand_aliasing={{}: (5, {})} | custom-call | flops 34359738368 | bytes 83886080 | tf_op jit(solution)/shard_map/pallas_call | solution.py:167
  349.4 37.4 %all-gather.8.cloned.1.call-done.refs_2_ = f32[1024,32,128]{2,1,0:T(8,128)} async-done(((f32[32,32,128]{2,1,0:T(8,128)}), f32[1024,32,128]{2,1,0:T(8,128)}) %all-gather.8.cloned.1.call-update) | async-done | bytes 16777232 | tf_op jit(solution)/shard_map/all_gather | solution.py:331
  386.8 74.3 %shard_map.102.refs_5_ = f32[256,4,64,128]{3,2,1,0:T(8,128)} custom-call(s32[1024]{0:T(1024)} %reshape_squeeze.13.refs_0_, s32[32]{0:T(128)} %slice_reduce_fusion.refs_1_, f32[1024,32,128]{2,1,0:T(8,128)} %all-gather.8.cloned.1.call-done.refs_2_, bf16[256,512]{1,0:T(8,128)(2,1)} %maximum_maximum_fusion.refs_3_, ...), custom_call_target="tpu_custom_call", output_to_operand_aliasing={{}: (5, {})} | custom-call | flops 34359738368 | bytes 83886080 | tf_op jit(solution)/shard_map/pallas_call | solution.py:167
  461.1 41.6 %all-gather.6.cloned.1.call-done.refs_2_ = f32[1024,32,128]{2,1,0:T(8,128)} async-done(((f32[32,32,128]{2,1,0:T(8,128)}), f32[1024,32,128]{2,1,0:T(8,128)}) %all-gather.6.cloned.1.call-update) | async-done | bytes 16777232 | tf_op jit(solution)/shard_map/all_gather | solution.py:331
  502.7 52.6 %shard_map.103.refs_0_ = f32[256,4,64,128]{3,2,1,0:T(8,128)} custom-call(s32[1024]{0:T(1024)} %reshape_squeeze.12.refs_0_, s32[32]{0:T(128)} %slice_reduce_fusion.refs_1_, f32[1024,32,128]{2,1,0:T(8,128)} %all-gather.6.cloned.1.call-done.refs_2_, bf16[256,512]{1,0:T(8,128)(2,1)} %maximum_maximum_fusion.refs_3_, ...), custom_call_target="tpu_custom_call", output_to_operand_aliasing={{}: (5, {})} | custom-call | flops 34359738368 | bytes 83886080 | tf_op jit(solution)/shard_map/pallas_call | solution.py:167
  555.3 94.1 %shard_map.104 = f32[2,256,8192]{2,1,0:T(8,128)} custom-call(f32[256,4,64,128]{3,2,1,0:T(8,128)} %shard_map.103.refs_0_, bf16[32,2,256,768]{3,2,1,0:T(8,128)(2,1)} %pad_maximum_fusion.1.refs_1_), custom_call_target="tpu_custom_call" | custom-call | flops 25769803776 | bytes 100663296 | tf_op jit(solution)/shard_map/pallas_call | solution.py:277
  (49 shorter events, 6.0 us)
Async XLA Ops:
  6.5 16.9 %copy-start.2 = (s32[128]{0:T(128)S(1)}, s32[128]{0:T(128)}, u32[]{:S(2)}) copy-start(s32[128]{0:T(128)} %param.14) | copy-start | bytes 1540
  6.5 16.9 %copy-start.1 = (f32[8]{0:T(128)S(1)}, f32[8]{0:T(128)}, u32[]{:S(2)}) copy-start(f32[8]{0:T(128)} %param.17) | copy-start | bytes 100
  6.5 148.1 %all-gather.12.cloned.1.call-start = ((), (), s32[]{:S(2)}) async-start(), calls=%async_computation.3 | async-start | bytes 17301504 | tf_op jit(solution)/shard_map/all_gather | solution.py:331
  24.6 3.5 slice-start
  25.4 2.9 slice-start.1
  28.3 4.9 slice-start.2
  30.8 2.4 slice-start.3
  35.5 4.0 copy-start
  36.6 234.1 %all-gather.10.cloned.1.call-start = ((), (), s32[]{:S(2)}) async-start(), calls=%async_computation.2 | async-start | bytes 17301504 | tf_op jit(solution)/shard_map/all_gather | solution.py:331
  37.6 349.2 %all-gather.8.cloned.1.call-start = ((), (), s32[]{:S(2)}) async-start(), calls=%async_computation.1 | async-start | bytes 17301504 | tf_op jit(solution)/shard_map/all_gather | solution.py:331
  38.5 464.2 %all-gather.6.cloned.1.call-start = ((), (), s32[]{:S(2)}) async-start(), calls=%async_computation | async-start | bytes 17301504 | tf_op jit(solution)/shard_map/all_gather | solution.py:331
Sparse Core Ops, SparseCore 0:
  36.7 117.8 all-gather.11
  157.6 113.0 all-gather.9
  273.7 113.0 all-gather.7
  389.6 113.0 all-gather.5

commit v2 on v1

v2 whole, which is shorter than its diff:
```python
import math

import jax
import jax.numpy as jnp
import numpy as np
from jax import lax
from jax.experimental import pallas as pl
from jax.experimental.pallas import tpu as pltpu
from jax.sharding import PartitionSpec as P

G = 8192
SUB = 32
TILES = G // SUB
HALF = 2 * SUB
AXES = ("row", "col")
GROUP = 16
PAD = 8
VMEM_LIMIT = 60 * 1024 * 1024


def split(value):
    high = lax.reduce_precision(value, 8, 7)
    return high.astype(jnp.bfloat16), (value - high).astype(jnp.bfloat16)


def subgrid_table():
    index = np.arange(SUB)
    k = np.arange(SUB // 2)
    u = np.stack([k, np.where(k == 0, SUB // 2, SUB - k)], axis=1)
    turns = (
        index[:, None, None, None, None] * u[None, None, :, :, None]
        + index[None, :, None, None, None] * index[None, None, None, None, :]
    ) % SUB
    wave = np.exp(-2j * np.pi / SUB * turns) / SUB
    table = np.zeros((2, SUB, SUB, SUB // 2, 2, 2, SUB))
    table[0, :, :, :, :, 0] = wave.real
    table[0, :, :, :, :, 1] = wave.imag
    table[1, :, :, :, :, 0] = -wave.imag
    table[1, :, :, :, :, 1] = wave.real
    table = table.reshape(2 * SUB * SUB, 2 * SUB * SUB).astype(np.float32)
    high = table.astype(jnp.bfloat16)
    low = (table - high.astype(np.float32)).astype(jnp.bfloat16)
    return high, low


def spectra_of(pixels, pairs, times, channels, valid, aterms, weights):
    slots = pixels.shape[0]
    first = aterms[pairs[:, 0], times].astype(jnp.float32)
    second = aterms[pairs[:, 1], times].astype(jnp.float32)
    gain_real = first[:, 0] * second[:, 0] + first[:, 1] * second[:, 1]
    gain_imag = first[:, 1] * second[:, 0] - first[:, 0] * second[:, 1]
    matches = channels[:, None] == jnp.arange(weights.shape[0], dtype=jnp.int32)[None, :]
    weight = jnp.sum(jnp.where(matches, weights[None, :], 0.0), axis=1)
    weight = jnp.where(valid, weight, 0.0)[:, None, None]
    real = (pixels[:, 0] * gain_real - pixels[:, 1] * gain_imag) * weight
    imag = (pixels[:, 0] * gain_imag + pixels[:, 1] * gain_real) * weight
    table_high, table_low = subgrid_table()
    dot = lambda left, right: jnp.dot(left, right, preferred_element_type=jnp.float32)
    spectra = []
    for feed in range(2):
        high, low = split(jnp.concatenate([real[:, feed], imag[:, feed]], axis=1))
        out = dot(high, table_high) + dot(low, table_high) + dot(high, table_low)
        spectra.append(out.reshape(slots, SUB // 2, 128))
    return spectra


def phases(turns, modulus):
    angle = (2.0 * math.pi / modulus) * (turns % modulus).astype(jnp.float32)
    return jnp.cos(angle), jnp.sin(angle)


def column_tables(first_m, lanes):
    m = first_m + jnp.arange(lanes, dtype=jnp.int32)
    cos, sin = phases(jnp.arange(SUB, dtype=jnp.int32)[:, None] * m[None, :], G)
    table = jnp.concatenate(
        [jnp.concatenate([cos, -sin], axis=1), jnp.concatenate([sin, cos], axis=1)], axis=0
    )
    high, low = split(table)
    table = jnp.concatenate([high, high, low, jnp.zeros_like(high)], axis=0)
    cos, sin = phases(jnp.arange(TILES, dtype=jnp.int32)[:, None] * m[None, :], TILES)
    return table, jnp.concatenate([cos, -sin], axis=1).reshape(TILES, 2 * lanes // 128, 128)


def row_table():
    b = jnp.arange(TILES, dtype=jnp.int32)
    k = jnp.arange(SUB // 2 + 1, dtype=jnp.int32)
    cos_r, sin_r = phases(b[:, None] * b[None, :], TILES)
    cos_k, sin_k = phases(k[:, None] * b[None, :], G)
    cos = cos_r[None] * cos_k[:, :, None] - sin_r[None] * sin_k[:, :, None]
    sin = sin_r[None] * cos_k[:, :, None] + cos_r[None] * sin_k[:, :, None]
    upper = jnp.concatenate([cos, sin], axis=2)
    lower = jnp.concatenate([-sin, cos], axis=2)
    lower = jnp.concatenate([upper[SUB // 2 :], lower[1 : SUB // 2]], axis=0)
    high, low = split(jnp.concatenate([upper[: SUB // 2], lower], axis=1))
    return jnp.stack([high, low], axis=1)


def feed_kernel(codes, counts, *refs, units, unit_slots, first, last, feed, lanes, wanted, scale):
    arrays = len(units)
    parts = refs[:arrays]
    table_ref, turn_ref, row_ref, held_ref, _, rows_out, image, total, blocks, mid, planes, slab = refs[
        arrays : arrays + 12
    ]
    sem, block_sems, sems = refs[arrays + 12 :]
    step = pl.program_id(0)
    tiles = 2 * lanes // 128
    side_rows = SUB // 2
    is_low = lax.broadcasted_iota(jnp.int32, (GROUP * side_rows, 128), 1) < HALF

    def add_group(unit, start):
        x = blocks[unit % 2, pl.ds(start, GROUP)].reshape(GROUP * side_rows, 128)
        high = x.astype(jnp.bfloat16).astype(jnp.float32)
        low = x - high
        high_turned = pltpu.roll(high, HALF, 1)
        low_turned = pltpu.roll(low, HALF, 1)
        sides = (
            (jnp.where(is_low, high, low_turned), high),
            (jnp.where(is_low, high_turned, low), high_turned),
        )
        left = jnp.concatenate(
            [
                jnp.concatenate([mixed.astype(jnp.bfloat16), other.astype(jnp.bfloat16)], axis=1)
                for mixed, other in sides
            ],
            axis=0,
        )
        mid[...] = jnp.dot(left, table_ref[...], preferred_element_type=jnp.float32)
        for item in range(GROUP):
            code = codes[unit, start + item]
            row = code // TILES
            turns = turn_ref[code % TILES]
            held, added = [], []
            for side, at_row in enumerate((row, TILES - 1 - row)):
                begin = (side * GROUP + item) * side_rows
                for tile in range(tiles // 2):
                    here = slice(tile * 128, (tile + 1) * 128)
                    there = slice(lanes + tile * 128, lanes + (tile + 1) * 128)
                    turn_real = turns[tile : tile + 1]
                    turn_imag = turns[tiles // 2 + tile : tiles // 2 + tile + 1]
                    real = mid[begin : begin + side_rows, here]
                    imag = mid[begin : begin + side_rows, there]
                    new_real = real * turn_real - imag * turn_imag
                    new_imag = real * turn_imag + imag * turn_real
                    for part, new in enumerate((new_real, new_imag if side == 0 else -new_imag)):
                        first_row = (part * (tiles // 2) + tile) * SUB + side * side_rows
                        place = (at_row, slice(first_row, first_row + side_rows))
                        held.append(place)
                        added.append(total[place] + new)
            for place, value in zip(held, added):
                total[place] = value

    def fetch(unit):
        offset = 0
        for part, count in zip(parts, units):
            inside = jnp.logical_and(unit >= offset, unit < offset + count)

            @pl.when(inside)
            def _(part=part, offset=offset):
                pltpu.make_async_copy(
                    part.at[pl.ds((unit - offset) * (unit_slots + 1), unit_slots)],
                    blocks.at[unit % 2],
                    block_sems.at[unit % 2],
                ).start()

            offset += count

    @pl.when(step == 0)
    def _():
        fetch(0)
        if first:
            total[...] = jnp.zeros_like(total)
        else:
            copy = pltpu.make_async_copy(held_ref, total, sem)
            copy.start()
            copy.wait()

        def add_unit(unit, carry):
            @pl.when(unit + 1 < sum(units))
            def _():
                fetch(unit + 1)

            pltpu.make_async_copy(
                parts[0].at[pl.ds(0, unit_slots)], blocks.at[unit % 2], block_sems.at[unit % 2]
            ).wait()

            def one(group, carry):
                add_group(unit, group * GROUP)
                return carry

            lax.fori_loop(0, (counts[unit] + GROUP - 1) // GROUP, one, 0)
            return carry

        lax.fori_loop(0, sum(units), add_unit, 0)

    if not last:

        copy = pltpu.make_async_copy(total, rows_out, sem)
        copy.start()
        copy.wait()
        return

    k = step - 1
    stride = tiles * SUB + PAD
    rows = total.reshape(TILES * stride, 128)

    def take(part, side):
        row = part * (tiles // 2) * SUB + side * side_rows + k
        pieces = [rows[pl.ds(row + tile * SUB, TILES, stride), :] for tile in range(tiles // 2)]
        return jnp.concatenate(pieces, axis=1)

    def transform(data, low_row, high_row):
        high = data.astype(jnp.bfloat16)
        low = (data - high.astype(jnp.float32)).astype(jnp.bfloat16)
        dot = lambda left, right: jnp.dot(left, right, preferred_element_type=jnp.float32)
        table_high = row_ref[0, 0, low_row:high_row]
        table_low = row_ref[0, 1, low_row:high_row]
        return dot(table_high, high) + dot(table_low, high) + dot(table_high, low)

    @pl.when(k == 0)
    def _():
        for side in range(2):
            data = jnp.concatenate([take(0, side), take(1, side)], axis=0)
            planes[side] = transform(data, side * TILES, (side + 1) * TILES)

    @pl.when(k > 0)
    def _():
        data = jnp.concatenate([take(part, 0) + take(part, 1) for part in range(2)], axis=0)
        out = transform(data, 0, 2 * TILES)
        planes[2 * k] = out[:TILES]
        planes[2 * k + 1] = out[TILES:]

    @pl.when(k == SUB // 2 - 1)
    def _():
        def last_stage(b_tile, carry):
            where = pl.ds(pl.multiple_of(b_tile * 8, 8), 8)
            for lane in range(lanes // 128):
                at = slice(lane * 128, (lane + 1) * 128)
                real = [planes[2 * j, where, at] for j in range(SUB // 2)]
                imag = [None] + [planes[2 * j + 1, where, at] for j in range(1, SUB // 2)] + [None]
                real.append(planes[1, where, at])
                for a, value in enumerate(real_transform(real, imag, SUB)):
                    planes[a, where, at] = value * scale
            return carry

        lax.fori_loop(0, TILES // 8, last_stage, 0)
        copies = []
        for a in range(SUB):
            at = slice(a * TILES, (a + 1) * TILES)
            slab[:, at] = planes[a].T[:wanted]
            copies.append(
                pltpu.make_async_copy(slab.at[:, at], image.at[feed, :, at], sems.at[a])
            )
            copies[-1].start()
        for copy in copies:
            copy.wait()


def add_feed(parts, codes, counts, tables, held, image, last, feed, lanes, wanted, scale):
    table, turn, row = tables
    unit_slots = codes.shape[1]
    units = [part.shape[0] // (unit_slots + 1) for part in parts]
    arrays = len(parts)
    shape = (TILES, 2 * lanes // 128 * SUB + PAD, 128)
    first = held is None
    blank = image is None
    if first:
        held = jnp.zeros((8, 128), jnp.float32)
    if blank:
        image = jnp.zeros((8, 128), jnp.float32)
    aliases = {}
    if not first and not last:
        aliases[2 + arrays + 3] = 0
    if not blank:
        aliases[2 + arrays + 4] = 1
    any_spec = pl.BlockSpec(memory_space=pl.ANY)

    def kernel(*refs):
        feed_kernel(
            *refs,
            units=units,
            unit_slots=unit_slots,
            first=first,
            last=last,
            feed=feed,
            lanes=lanes,
            wanted=wanted,
            scale=scale,
        )

    return pl.pallas_call(
        kernel,
        out_shape=[
            jax.ShapeDtypeStruct((8, 128) if last else shape, jnp.float32),
            jax.ShapeDtypeStruct((2, wanted, G), jnp.float32),
        ],
        grid_spec=pltpu.PrefetchScalarGridSpec(
            num_scalar_prefetch=2,
            grid=(1 + (SUB // 2 if last else 0),),
            in_specs=[any_spec] * arrays
            + [
                pl.BlockSpec(table.shape, lambda i, *_: (0, 0)),
                pl.BlockSpec(turn.shape, lambda i, *_: (0, 0, 0)),
                pl.BlockSpec((1,) + row.shape[1:], lambda i, *_: (jnp.maximum(i - 1, 0), 0, 0, 0)),
                any_spec,
                any_spec,
            ],
            out_specs=[any_spec, any_spec],
            scratch_shapes=[
                pltpu.VMEM(shape, jnp.float32),
                pltpu.VMEM((2, unit_slots, SUB // 2, 128), jnp.float32),
                pltpu.VMEM((GROUP * SUB, 2 * lanes), jnp.float32),
                pltpu.VMEM((SUB, TILES, lanes), jnp.float32),
                pltpu.VMEM((wanted, G), jnp.float32),
                pltpu.SemaphoreType.DMA,
                pltpu.SemaphoreType.DMA((2,)),
                pltpu.SemaphoreType.DMA((SUB,)),
            ],
        ),
        input_output_aliases=aliases,
        compiler_params=pltpu.CompilerParams(
            vmem_limit_bytes=VMEM_LIMIT, dimension_semantics=("arbitrary",)
        ),
        cost_estimate=pl.CostEstimate(
            flops=sum(units) * unit_slots * SUB * 256 * 2 * lanes * 2 * 2,
            bytes_accessed=sum(part.size for part in parts) * 4 + math.prod(shape) * 4,
            transcendentals=0,
        ),
    )(codes, counts, *parts, table, turn, row, held, image)


def real_transform(real, imag, size):
    if size == 2:
        return [real[0] + real[1], real[0] - real[1]]
    half = size // 2
    quarter = half // 2
    even = real_transform(real[::2], imag[::2], half)
    odd_indices = list(range(1, half, 2))

    def total(terms, a, wave):
        result = None
        for k in odd_indices:
            factor = wave(2.0 * math.pi * k * a / size)
            if abs(factor) < 1e-9:
                continue
            term = terms[k] * factor if abs(factor - 1.0) > 1e-9 else terms[k]
            result = term if result is None else result + term
        return result

    cosines = [total(real, a, math.cos) for a in range(quarter)] + [None]
    sines = [None] + [total(imag, a, math.sin) for a in range(1, quarter + 1)]
    odd = [None] * half
    for a in range(quarter + 1):
        if cosines[a] is None:
            odd[a] = sines[a]
        elif sines[a] is None:
            odd[a] = cosines[a]
        else:
            odd[a] = cosines[a] + sines[a]
            odd[half - a] = sines[a] - cosines[a]
    return [even[a] + odd[a] for a in range(half)] + [even[a] - odd[a] for a in range(half)]


def local(
    subgrid_pixels,
    tile_offsets,
    station_pairs,
    time_blocks,
    channel_blocks,
    valid_counts,
    aterms,
    channel_weights,
):
    devices = lax.axis_size("row") * lax.axis_size("col")
    slots = subgrid_pixels.shape[0]
    wanted = G // devices
    lanes = max(wanted, 128)
    first_m = (lax.axis_index("row") * lax.axis_size("col") + lax.axis_index("col")) * wanted
    valid = jnp.arange(slots, dtype=jnp.int32) < valid_counts[0]
    codes = jnp.where(valid, tile_offsets[:, 0] * TILES + tile_offsets[:, 1], 0)

    spectra = spectra_of(
        subgrid_pixels, station_pairs, time_blocks, channel_blocks, valid, aterms, channel_weights
    )
    tables = column_tables(first_m, lanes) + (row_table(),)
    scale = 1.0 / (SUB * math.sqrt(slots * devices))

    def gather(feed, start, stop):
        remaining = jnp.clip(valid_counts - start, 0, stop - start)
        details = jnp.concatenate([codes[start:stop], remaining]).astype(jnp.float32)
        details = jnp.pad(details, (0, 128 * SUB // 2 - details.shape[0]))
        details = details.reshape(1, SUB // 2, 128)
        own = jnp.concatenate([spectra[feed][start:stop], details], axis=0)
        return lax.all_gather(own, AXES, tiled=True)

    def add(parts, rows, image, last, feed):
        size = parts[0].shape[0] // devices
        notes = [
            part.reshape(-1, size, SUB // 2, 128)[:, size - 1, 0, :size] for part in parts
        ]
        notes = jnp.concatenate(notes, axis=0).astype(jnp.int32)
        return add_feed(
            parts,
            notes[:, : size - 1],
            notes[:, size - 1],
            tables,
            rows,
            image,
            last,
            feed,
            lanes,
            wanted,
            scale,
        )

    image = None
    if devices <= 32:
        half, late = slots // 2, slots * 3 // 4
        ends = [[(0, half), (half, slots)], [(0, half), (half, late), (late, slots)]]
        pieces = [[gather(feed, *span) for span in spans] for feed, spans in enumerate(ends)]
        for feed in range(2):
            rows = None
            for index, piece in enumerate(pieces[feed]):
                if image is None:
                    piece, tables = lax.optimization_barrier((piece, tables))
                else:
                    piece, image = lax.optimization_barrier((piece, image))
                rows, image = add([piece], rows, image, index == len(pieces[feed]) - 1, feed)
        return image
    size = slots * 32 // devices
    for feed in range(2):
        rows = None
        for start in range(0, slots, size):
            if image is not None:
                spectra[feed], image = lax.optimization_barrier((spectra[feed], image))
            part = gather(feed, start, start + size)
            rows, image = add([part], rows, image, start + size == slots, feed)
    return image


def solution(mesh):
    in_specs = (
        P(AXES, None, None, None),
        P(AXES, None),
        P(AXES, None),
        P(AXES),
        P(AXES),
        P(AXES),
        P(),
        P(),
    )
    out_specs = P(None, AXES, None)
    return jax.shard_map(local, mesh=mesh, in_specs=in_specs, out_specs=out_specs, check_vma=False)
```

time: 658 us -> 618 us (0.939)
  blocking collectives: 70.7 us -> 0 us
  waiting for transfers between devices: 127 us -> 194 us
  Pallas kernels: 372 us -> 324 us
  other arithmetic: 37.7 us -> 47.7 us
    all_gather x1 -> x0, blocking collectives: 70.7 us -> none  [local(): lax.all_gather(small, AXES, tiled=True).reshape(devices, slots + 128)]
    all_gather x4 -> x5, waiting for transfers between devices: 126 us -> 194 us  [gather(): return lax.all_gather(own, AXES, tiled=True)]
    pallas_call x5, Pallas kernels: 372 us -> 324 us  [add_feed(): pl.pallas_call(kernel, out_shape=[jax.ShapeDtypeStruct((8, 128) if last e...]
    concatenate x2 -> x6, other arithmetic: 9.07 us -> 17.7 us  [the longest x1 13.3 us: row_table(): high, low = split(jnp.concatenate([upper[:SUB // 2], lower], axis=1))]
  transfers between devices with their start and end apart: 4 -> 5, of which waited for: 4 -> 5; matrix products, arithmetic and copies ran while one was open for 7% -> 8% of each run, Pallas kernels for 34% -> 43%
where the time goes in v2:
time: 618 us; the launch traced here: 616 us
  Pallas kernels  324 us (52%)
  waiting for transfers between devices  194 us (31%)
  other arithmetic  47.7 us (8%)
  local copies, waits for them, and re-layouts  27.3 us (4%)
  between operations  14.3 us (2%)
  matrix products  7.84 us (1%)
    pallas_call x5, Pallas kernels, add_feed(): pl.pallas_call(kernel, out_shape=[jax.ShapeDtypeStruct((8, 128) if last e...  324 us
    all_gather x5, waiting for transfers between devices, gather(): return lax.all_gather(own, AXES, tiled=True)  194 us
    concatenate x1, other arithmetic, row_table(): high, low = split(jnp.concatenate([upper[:SUB // 2], lower], axis=1))  13.3 us
  transfers between devices with their start and end apart: 5, of which 5 were waited for; matrix products, arithmetic and copies ran while one was open for 8% of the time, Pallas kernels for 43%

profile of v2, /device:TPU:0, one launch (start us, length us, event | category | flops | bytes accessed | tf_op | source)
XLA Modules:
  0.0 615.5 jit_solution(14434012831768508454)
XLA Ops:
  8.0 6.2 %gather_fusion = bf16[128,2,2,1024]{3,2,1,0:T(2,128)(2,1)S(1)} fusion(bf16[512,2,2,2,1024]{4,3,2,1,0:T(2,128)(2,1)} %param.16, s32[128]{0:T(128)S(1)} %get-tuple-element.71), kind=kCustom, calls=%fused_computation | custom fusion | bytes 2098176 | tf_op jit(solution)/shard_map/gather | solution.py:48
  14.2 6.2 %gather_fusion.1 = bf16[128,2,2,1024]{3,2,1,0:T(2,128)(2,1)S(1)} fusion(bf16[512,2,2,2,1024]{4,3,2,1,0:T(2,128)(2,1)} %param.16, s32[128]{0:T(128)S(1)} %get-tuple-element.72), kind=kCustom, calls=%fused_computation.1 | custom fusion | bytes 2098176 | tf_op jit(solution)/shard_map/gather | solution.py:49
  20.4 2.3 fusion.61
  23.6 1.1 bitcast_multiply_fusion.1
  25.7 1.5 slice-done.1
  27.3 1.3 fusion.40
  28.6 1.3 convolution_add_fusion.1
  29.9 1.1 slice-done.3
  31.0 1.3 convolution_add_fusion
  32.7 1.3 fusion.39
  34.0 1.3 convolution_add_fusion.3
  35.3 1.3 convolution_add_fusion.2
  36.9 1.1 pad_maximum_fusion.5
  42.1 1.0 fusion.23
  43.3 3.8 fusion.21
  47.1 1.0 pad_maximum_fusion.8.refs_4_
  49.0 5.6 multiply_add_fusion
  54.6 13.3 %fusion.2 = (f32[16,1,256,512]{3,2,1,0:T(8,128)}, f32[16,1,256,512]{3,2,1,0:T(8,128)}) fusion(f32[17,256,256]{2,1,0:T(8,128)} %get-tuple-element.64, f32[17,256,256]{2,1,0:T(8,128)} %get-tuple-element.62, f32[17,256,256]{2,1,0:T(8,128)} %get-tuple-element.63), kind=kLoop, calls=%fused_computation.10 | loop fusion | flops 14680064 | bytes 30146560 | tf_op jit(solution)/shard_map/concatenate | solution.py:94
  67.9 7.8 %reduce-precision_convert_fusion = (bf16[16,1,512,512]{3,2,1,0:T(8,128)(2,1)S(1)}, bf16[16,1,512,512]{3,2,1,0:T(8,128)(2,1)S(1)}) fusion(f32[16,1,256,512]{3,2,1,0:T(8,128)} %get-tuple-element.51, f32[16,1,256,512]{3,2,1,0:T(8,128)} %get-tuple-element.50), kind=kLoop, calls=%fused_computation.3 | loop fusion | flops 20971520 | bytes 33554432 | tf_op jit(solution)/shard_map/convert_element_type | solution.py:23
  75.6 6.9 %pad_maximum_fusion.1.refs_5_ = bf16[16,2,512,512]{3,2,1,0:T(8,128)(2,1)} fusion(bf16[16,1,512,512]{3,2,1,0:T(8,128)(2,1)S(1)} %get-tuple-element.49, bf16[16,1,512,512]{3,2,1,0:T(8,128)(2,1)S(1)} %get-tuple-element.48), kind=kLoop, calls=%fused_computation.6 | loop fusion | flops 8388608 | bytes 33554432 | tf_op jit(solution)/shard_map/stack | solution.py:95
  82.6 74.3 %all-gather.14.cloned.1.call-done.refs_2_ = f32[2080,16,128]{2,1,0:T(8,128)} async-done(((f32[65,16,128]{2,1,0:T(8,128)}), f32[2080,16,128]{2,1,0:T(8,128)}) %all-gather.14.cloned.1.call-update) | async-done | bytes 17039376 | tf_op jit(solution)/shard_map/all_gather | solution.py:393
  156.9 0.9 slice.210
  159.1 72.9 %shard_map.100 = (f32[256,136,128]{2,1,0:T(8,128)}, f32[2,256,8192]{2,1,0:T(8,128)}) custom-call(s32[32,64]{1,0:T(8,128)} %bitcast.99, s32[32]{0:T(128)} %slice_reduce_fusion.4.refs_1_, f32[2080,16,128]{2,1,0:T(8,128)} %all-gather.14.cloned.1.call-done.refs_2_, bf16[256,512]{1,0:T(8,128)(2,1)} %maximum_maximum_fusion.refs_3_, ...), custom_call_target="tpu_custom_call" | custom-call | flops 34359738368 | bytes 34865152 | tf_op jit(solution)/shard_map/pallas_call | solution.py:290
  232.1 42.2 %all-gather.12.cloned.1.call-done.refs_2_ = f32[2080,16,128]{2,1,0:T(8,128)} async-done(((f32[65,16,128]{2,1,0:T(8,128)}), f32[2080,16,128]{2,1,0:T(8,128)}) %all-gather.12.cloned.1.call-update) | async-done | bytes 17039376 | tf_op jit(solution)/shard_map/all_gather | solution.py:393
  274.3 0.9 slice.213
  275.9 76.1 %shard_map.101 = (f32[8,128]{1,0:T(8,128)}, f32[2,256,8192]{2,1,0:T(8,128)}) custom-call(s32[32,64]{1,0:T(8,128)} %bitcast.97, s32[32]{0:T(128)} %slice_reduce_fusion.3.refs_1_, f32[2080,16,128]{2,1,0:T(8,128)} %all-gather.12.cloned.1.call-done.refs_2_, bf16[256,512]{1,0:T(8,128)(2,1)} %maximum_maximum_fusion.refs_3_, ...), custom_call_target="tpu_custom_call", output_to_operand_aliasing={{1}: (7, {})} | custom-call | flops 34359738368 | bytes 34865152 | tf_op jit(solution)/shard_map/pallas_call | solution.py:290
  352.1 39.4 %all-gather.10.cloned.1.call-done.refs_2_ = f32[2080,16,128]{2,1,0:T(8,128)} async-done(((f32[65,16,128]{2,1,0:T(8,128)}), f32[2080,16,128]{2,1,0:T(8,128)}) %all-gather.10.cloned.1.call-update) | async-done | bytes 17039376 | tf_op jit(solution)/shard_map/all_gather | solution.py:393
  393.1 72.9 %shard_map.102 = (f32[256,136,128]{2,1,0:T(8,128)}, f32[2,256,8192]{2,1,0:T(8,128)}) custom-call(s32[32,64]{1,0:T(8,128)} %bitcast.100, s32[32]{0:T(128)} %slice_reduce_fusion.2.refs_1_, f32[2080,16,128]{2,1,0:T(8,128)} %all-gather.10.cloned.1.call-done.refs_2_, bf16[256,512]{1,0:T(8,128)(2,1)} %maximum_maximum_fusion.refs_3_, ...), custom_call_target="tpu_custom_call", output_to_operand_aliasing={{1}: (7, {})} | custom-call | flops 34359738368 | bytes 34865152 | tf_op jit(solution)/shard_map/pallas_call | solution.py:290
  466.1 4.9 all-gather.8.cloned.1.call-done.refs_2_
  472.7 45.4 %shard_map.103 = (f32[256,136,128]{2,1,0:T(8,128)}, f32[2,256,8192]{2,1,0:T(8,128)}) custom-call(s32[32,32]{1,0:T(8,128)} %bitcast.98, s32[32]{0:T(128)} %slice_reduce_fusion.1.refs_1_, f32[1056,16,128]{2,1,0:T(8,128)} %all-gather.8.cloned.1.call-done.refs_2_, ...), custom_call_target="tpu_custom_call", output_to_operand_aliasing={{0}: (6, {}), {1}: (7, {})} | custom-call | flops 17179869184 | bytes 26476544 | tf_op jit(solution)/shard_map/pallas_call | solution.py:290
  518.1 32.9 %all-gather.6.cloned.1.call-done.refs_2_ = f32[1056,16,128]{2,1,0:T(8,128)} async-done(((f32[33,16,128]{2,1,0:T(8,128)}), f32[1056,16,128]{2,1,0:T(8,128)}) %all-gather.6.cloned.1.call-update) | async-done | bytes 8650768 | tf_op jit(solution)/shard_map/all_gather | solution.py:393
  552.6 56.4 %shard_map.104 = (f32[8,128]{1,0:T(8,128)}, f32[2,256,8192]{2,1,0:T(8,128)}) custom-call(s32[32,32]{1,0:T(8,128)} %bitcast.96, s32[32]{0:T(128)} %slice_reduce_fusion.refs_1_, f32[1056,16,128]{2,1,0:T(8,128)} %all-gather.6.cloned.1.call-done.refs_2_, bf16[256,512]{1,0:T(8,128)(2,1)} %maximum_maximum_fusion.refs_3_, ...), custom_call_target="tpu_custom_call", output_to_operand_aliasing={{1}: (7, {})} | custom-call | flops 17179869184 | bytes 26476544 | tf_op jit(solution)/shard_map/pallas_call | solution.py:290
  (84 shorter events, 15.3 us)
Async XLA Ops:
  6.5 16.1 %copy-start.7 = (s32[128]{0:T(128)S(1)}, s32[128]{0:T(128)}, u32[]{:S(2)}) copy-start(s32[128]{0:T(128)} %param.14) | copy-start | bytes 1540
  6.5 16.1 %copy-start.6 = (f32[8]{0:T(128)S(1)}, f32[8]{0:T(128)}, u32[]{:S(2)}) copy-start(f32[8]{0:T(128)} %param.17) | copy-start | bytes 100
  6.5 150.4 %all-gather.14.cloned.1.call-start = ((), (), s32[]{:S(2)}) async-start(), calls=%async_computation.4 | async-start | bytes 17571840 | tf_op jit(solution)/shard_map/all_gather | solution.py:393
  23.6 2.2 slice-start
  24.6 2.6 slice-start.1
  27.3 2.6 slice-start.2
  28.6 2.4 slice-start.3
  35.3 1.5 copy-start.5
  38.0 236.2 %all-gather.12.cloned.1.call-start = ((), (), s32[]{:S(2)}) async-start(), calls=%async_computation.3 | async-start | bytes 17571840 | tf_op jit(solution)/shard_map/all_gather | solution.py:393
  39.1 352.4 %all-gather.10.cloned.1.call-start = ((), (), s32[]{:S(2)}) async-start(), calls=%async_computation.2 | async-start | bytes 17571840 | tf_op jit(solution)/shard_map/all_gather | solution.py:393
  39.8 431.2 %all-gather.8.cloned.1.call-start = ((), (), s32[]{:S(2)}) async-start(), calls=%async_computation.1 | async-start | bytes 8921088 | tf_op jit(solution)/shard_map/all_gather | solution.py:393
  40.9 510.1 %all-gather.6.cloned.1.call-start = ((), (), s32[]{:S(2)}) async-start(), calls=%async_computation | async-start | bytes 8921088 | tf_op jit(solution)/shard_map/all_gather | solution.py:393
  157.8 1.3 copy-start.3
  275.2 0.7 copy-start.1
  392.3 0.8 copy-start.4
  471.9 0.8 copy-start.2
  551.9 0.7 copy-start
Sparse Core Ops, SparseCore 0:
  38.1 118.7 all-gather.13
  159.7 114.4 all-gather.11
  277.1 114.2 all-gather.9
  394.1 76.8 all-gather.7
  473.6 77.2 all-gather.5
